TPU v7x, 32 devices: a whole 2x2x4 slice. The times are simulated.
32 devices in a mesh: groups: 2 (over y), depth: 4 (over z), rays: 4 (over x, core).
Axes of the slice: x: 2, y: 2, z: 4, core: 2. Of those that a mesh axis runs over, the one named last changes fastest.
Arguments:
- brick_features: bfloat16 [16, 8, 4, 16384], P(None, ('groups', 'depth'), 'rays'), parts along dimension 1, may hold values from -6 to 6
- entry_cells: int32 [8, 4, 1024], P(('groups', 'depth'), 'rays'), parts along dimension 0, may hold values from 0 to 16368
- sample_counts: int32 [8, 4, 1024], P(('groups', 'depth'), 'rays'), parts along dimension 0, may hold values from 1 to 16, as said below
- brick_rank: int32 [8, 4], P(('groups', 'rays')), parts along dimension 0, may hold values from 0 to 3, each once within a row
- input_layer_weight: bfloat16 [16, 128], replicated, may hold values from -1.5 to 1.5
- second_weight: bfloat16 [128, 33], replicated, may hold values from -0.5 to 0.5
- conv_in: bfloat16 [9, 32, 128], replicated, may hold values from -0.375 to 0.375
- conv_mid: bfloat16 [9, 128, 128], replicated, may hold values from -0.1875 to 0.1875
- conv_out: bfloat16 [9, 128, 128], replicated, may hold values from -0.1875 to 0.1875
Outputs:
- frame: bfloat16 [128, 64, 128], P(('groups', 'depth'), 'rays'), parts along dimension 0
There are 2 independent parts, one for each index of `groups`. A program takes and returns all parts, laid end to end along the dimension named above; an argument that names none is the same for every part. Nothing has to cross between parts.
Inputs may be any that keep to these rules, and one draw needn't show every extreme that they name: `sample_counts`: each brick and strip has a level of at most 16; its rays take 1 to that level samples; some brick and strip reaches 16. `brick_rank`: each row is a permutation of the bricks.
All inputs are finite; a program needn't handle non-finite values.
Results may differ from a plain program's by a relative error of at most 0.015.
Values may be sent and summed in bfloat16 or wider, within the bound.
A program may use at most 64 MiB of HBM per device.

v0:
```python
import math
import jax
import jax.numpy as jnp
from jax import lax
from jax.sharding import PartitionSpec as P

SAMPLES = 16
ROWS_OWN = 16
COLS_DEV = 16


def padded_2(x, sides, width):
    for axis, dim in sides:
        size, length = (lax.axis_size(axis), x.shape[dim])
        up = [(i, (i + 1) % size) for i in range(size - 1)]
        down = [(j, i) for i, j in up]
        last = lax.slice_in_dim(x, length - width, length, axis=dim)
        first = lax.slice_in_dim(x, 0, width, axis=dim)
        before = lax.ppermute(last, axis, up)
        after = lax.ppermute(first, axis, down)
        x = jnp.concatenate([before, x, after], axis=dim)
    return x


def blend_sample_values(field, counts, bricks):
    step_len = 8.0 / (SAMPLES * bricks)
    slot_ids = jnp.arange(SAMPLES, dtype=jnp.int32)
    valid = (slot_ids[:, None] < counts[None, :]).astype(jnp.float32)
    optical = step_len * jax.nn.softplus(field[0]) * valid
    earlier = (slot_ids[:, None] > slot_ids[None, :]).astype(jnp.float32)
    before = jnp.dot(earlier, optical, precision=lax.Precision.HIGHEST)
    weights = jnp.exp(-before) * (1.0 - jnp.exp(-optical))
    colour = jnp.sum(weights[None] * field[1:], axis=1)
    return (colour, jnp.sum(optical, axis=0))


def convolve_valid(padded, weights):
    height = padded.shape[0] - 2
    width = padded.shape[1] - 2
    total = jnp.zeros((height * width, weights.shape[2]), jnp.float32)
    for tap in range(9):
        row_offset_shift, shift_col = divmod(tap, 3)
        window = padded[
            row_offset_shift : row_offset_shift + height, shift_col : shift_col + width
        ].reshape(height * width, -1)
        total = total + jnp.dot(window, weights[tap], preferred_element_type=jnp.float32)
    return total.reshape(height, width, weights.shape[2])


def border_padding(source):
    return padded_2(source, (("depth", 0), ("rays", 1)), 1)


def shards(
    brick_features,
    entry_cells,
    sample_counts,
    brick_rank,
    input_layer_weight,
    second_weight,
    conv_in,
    conv_mid,
    conv_out,
):
    bricks = lax.axis_size("depth")
    feat_count = brick_features.shape[0]
    cell_count = brick_features.shape[3]
    windows = cell_count // SAMPLES
    span = SAMPLES * feat_count
    table = (
        brick_features.reshape(feat_count, windows, SAMPLES)
        .transpose(1, 2, 0)
        .reshape(windows, span)
    )
    entries = entry_cells.reshape(-1)
    counts = sample_counts.reshape(-1)
    ranks = brick_rank.reshape(-1)
    total_rays = entries.shape[0]
    block = math.gcd(total_rays, 512)
    shift_bits = (SAMPLES - 1).bit_length()

    def march_block(operands):
        block_entries, block_counts = operands
        window_ids = block_entries // SAMPLES
        offset = block_entries - window_ids * SAMPLES
        following = jnp.minimum(window_ids + 1, windows - 1)
        paired = jnp.concatenate(
            [jnp.take(table, window_ids, axis=0), jnp.take(table, following, axis=0)], axis=1
        )
        for level in range(shift_bits):
            moved_by = (1 << level) * feat_count
            moved = jnp.concatenate(
                [paired[:, moved_by:], jnp.zeros((block, moved_by), paired.dtype)], axis=1
            )
            taken = (offset >> level & 1)[:, None] == 1
            paired = jnp.where(taken, moved, paired)
        probed_values = paired[:, :span].reshape(block, SAMPLES, feat_count)
        before_activation = jnp.einsum(
            "fh,isf->hsi", input_layer_weight, probed_values, preferred_element_type=jnp.float32
        )
        hidden = (
            jnp.maximum(before_activation, 0.0).astype(jnp.bfloat16).reshape(-1, SAMPLES * block)
        )
        field = jnp.einsum("ho,hn->on", second_weight, hidden, preferred_element_type=jnp.float32)
        return blend_sample_values(field.reshape(-1, SAMPLES, block), block_counts, bricks)

    colour_blocks, depth_blocks = lax.map(
        march_block, (entries.reshape(-1, block), counts.reshape(-1, block))
    )
    colour = jnp.transpose(colour_blocks, (1, 0, 2)).reshape(colour_blocks.shape[1], total_rays)
    depth_sum = depth_blocks.reshape(1, total_rays)
    all_depth = lax.all_gather(depth_sum, "depth", axis=0, tiled=True)
    my_rank = ranks[lax.axis_index("depth")]
    ahead = (ranks < my_rank).astype(jnp.float32)[None, :]
    front = jnp.dot(ahead, all_depth, precision=lax.Precision.HIGHEST)
    image = lax.psum_scatter(
        (colour * jnp.exp(-front)).astype(jnp.bfloat16), "depth", scatter_dimension=1, tiled=True
    ).astype(jnp.float32)
    image = image.reshape(-1, ROWS_OWN, COLS_DEV).transpose(1, 2, 0).astype(jnp.bfloat16)
    first = jnp.maximum(convolve_valid(border_padding(image), conv_in), 0.0).astype(jnp.bfloat16)
    second = jnp.maximum(convolve_valid(border_padding(first), conv_mid), 0.0).astype(jnp.bfloat16)
    frame = convolve_valid(border_padding(second), conv_out).astype(jnp.bfloat16)
    return frame


def solution(mesh):
    placed = (
        P(None, ("groups", "depth"), "rays", None),
        P(("groups", "depth"), "rays", None),
        P(("groups", "depth"), "rays", None),
        P(("groups", "rays"), None),
        P(),
        P(),
        P(),
        P(),
        P(),
    )
    return jax.shard_map(
        shards,
        mesh=mesh,
        in_specs=placed,
        out_specs=P(("groups", "depth"), "rays", None),
        check_vma=False,
    )
```

profile of v0, /device:TPU:1, one launch (start us, length us, event | category | flops | bytes accessed | tf_op | source)
XLA Modules:
  0.0 133.9 jit_solution(3947614905401499600)
XLA Ops:
  7.1 1.3 reduce.10
  8.3 1.3 reduce.11
  9.6 5.4 %reshape.274 = bf16[16,1024,16]{2,1,0:T(8,128)(2,1)} reshape(bf16[16,1,1,16384]{3,0,2,1:T(8,128)(2,1)} %param.13) | data formatting | bytes 1048576 | tf_op jit(solution)/shard_map/reshape | solution.py:71
  15.1 3.7 %copy.18 = bf16[1024,16,16]{0,2,1:T(8,128)(2,1)S(1)} copy(bf16[1024,16,16]{1,0,2:T(8,128)(2,1)} %bitcast.218) | data formatting | bytes 1048576 | tf_op jit(solution)/shard_map/transpose | solution.py:72
  19.0 19.6 %while.14 = (s32[]{:T(128)}, f32[2,32,512]{2,1,0:T(8,128)S(1)}, f32[2,512]{1,0:T(2,128)S(1)}, s32[2,512]{1,0:T(2,128)S(1)}, s32[2,512]{1,0:T(2,128)S(1)}, /*inde...) while((s32[]{:T(128)}, f32[2,32,512]{2,1,0:T(8,128)S(1)}, ...), condition=%wide.region_3.5_spmd, body=%wide.region_0.4_spmd.sunk | while | flops 110472448 | bytes 23171440 | solution.py:107
  19.1 2.0 %gather_fusion.1 = bf16[512,256]{1,0:T(8,128)(2,1)S(1)} fusion(bf16[1024,256]{1,0:T(8,128)(2,1)S(1)} %get-tuple-element.298, s32[1024]{0:T(1024)S(1)} %pad_clamp_fusion.5), kind=kCustom, calls=%fused_computation.clone.clone.1 | custom fusion | bytes 526336 | tf_op jit(solution)/shard_map/while/body/eval_jaxpr/jit(_take)/gather | solution.py:88
  21.2 2.0 %gather_fusion = bf16[512,256]{1,0:T(8,128)(2,1)S(1)} fusion(bf16[1024,256]{1,0:T(8,128)(2,1)S(1)} %get-tuple-element.298, s32[1024]{0:T(1024)S(1)} %pad_clamp_fusion.4), kind=kCustom, calls=%fused_computation.1.clone.clone.1 | custom fusion | bytes 526336 | tf_op jit(solution)/shard_map/while/body/eval_jaxpr/jit(_take)/gather | solution.py:88
  26.1 1.3 convolution_bitcast_fusion.2
  28.9 2.0 %gather_fusion.1 = bf16[512,256]{1,0:T(8,128)(2,1)S(1)} fusion(bf16[1024,256]{1,0:T(8,128)(2,1)S(1)} %get-tuple-element.298, s32[1024]{0:T(1024)S(1)} %pad_clamp_fusion.5), kind=kCustom, calls=%fused_computation.clone.clone.1 | custom fusion | bytes 526336 | tf_op jit(solution)/shard_map/while/body/eval_jaxpr/jit(_take)/gather | solution.py:88
  31.0 2.0 %gather_fusion = bf16[512,256]{1,0:T(8,128)(2,1)S(1)} fusion(bf16[1024,256]{1,0:T(8,128)(2,1)S(1)} %get-tuple-element.298, s32[1024]{0:T(1024)S(1)} %pad_clamp_fusion.4), kind=kCustom, calls=%fused_computation.1.clone.clone.1 | custom fusion | bytes 526336 | tf_op jit(solution)/shard_map/while/body/eval_jaxpr/jit(_take)/gather | solution.py:88
  35.9 1.3 convolution_bitcast_fusion.2
  38.6 11.3 %all-gather = f32[4,1,1024]{2,1,0:T(1,128)S(1)} all-gather(f32[1,1,1024]{2,1,0:T(1,128)S(1)} %reshape.322), channel_id=1, replica_groups=mesh['groups'=2,'depth'=4,'rays'=4] {'depth'}, dimensions={0}, use_global_device_ids=true | all-gather | bytes 20480 | tf_op jit(solution)/shard_map/all_gather | solution.py:112
  52.0 20.8 %reduce-scatter.2.cloned.1.call-done = bf16[32,256]{1,0:T(8,128)(2,1)} async-done(((bf16[32,1024]{1,0:T(8,128)(2,1)}), bf16[32,256]{1,0:T(8,128)(2,1)}) %reduce-scatter.2.cloned.1.call-update) | async-done | bytes 16400 | tf_op jit(solution)/shard_map/reduce_scatter | solution.py:116
  72.8 0.8 copy.21
  73.6 1.3 collective-permute-start
  74.9 1.3 collective-permute-start.1
  76.2 3.0 %collective-permute-done.1 = bf16[1,16,32]{2,1,0:T(8,128)(2,1)S(1)} collective-permute-done((bf16[1,16,32]{2,1,0:T(8,128)(2,1)S(1)}, bf16[1,16,32]{2,1,0:T(8,128)(2,1)S(1)}, u32[]{:S(2)}, u32[]{:S(2)}) %collective-permute-start.1) | collective-permute-done | bytes 1056 | tf_op jit(solution)/shard_map/ppermute | solution.py:20
  79.3 7.1 %collective-permute-start.2 = (bf16[18,1,32]{2,1,0:T(2,128)(2,1)S(1)}, bf16[18,1,32]{2,1,0:T(2,128)(2,1)S(1)}, u32[]{:S(2)}, u32[]{:S(2)}) collective-permute-start(bf16[18,1,32]{2,1,0:T(2,128)(2,1)S(1)} %get-tuple-element.183), channel_id=1, source_target_pairs={{0,1},{1,2},{2,3},{4,5},{5,6},{6,7},{8,9},{9,10},{10,11},{12,13},{... | collective-permute-start | bytes 3464 | tf_op jit(solution)/shard_map/ppermute | solution.py:19
  86.4 1.9 %collective-permute-start.3 = (bf16[18,1,32]{2,1,0:T(2,128)(2,1)S(1)}, bf16[18,1,32]{2,1,0:T(2,128)(2,1)S(1)}, u32[]{:S(2)}, u32[]{:S(2)}) collective-permute-start(bf16[18,1,32]{2,1,0:T(2,128)(2,1)S(1)} %get-tuple-element.184), channel_id=1, source_target_pairs={{1,0},{2,1},{3,2},{5,4},{6,5},{7,6},{9,8},{10,9},{11,10},{13,12},{... | collective-permute-start | bytes 3464 | tf_op jit(solution)/shard_map/ppermute | solution.py:20
  88.5 2.9 %collective-permute-done.3 = bf16[18,1,32]{2,1,0:T(2,128)(2,1)S(1)} collective-permute-done((bf16[18,1,32]{2,1,0:T(2,128)(2,1)S(1)}, bf16[18,1,32]{2,1,0:T(2,128)(2,1)S(1)}, u32[]{:S(2)}, u32[]{:S(2)}) %collective-permute-start.3) | collective-permute-done | bytes 1184 | tf_op jit(solution)/shard_map/ppermute | solution.py:20
  92.7 3.4 %collective-permute-start.4 = (bf16[1,16,128]{2,1,0:T(8,128)(2,1)S(1)}, bf16[1,16,128]{2,1,0:T(8,128)(2,1)S(1)}, u32[]{:S(2)}, u32[]{:S(2)}) collective-permute-start(bf16[1,16,128]{2,1,0:T(8,128)(2,1)S(1)} %get-tuple-element.191), channel_id=1, source_target_pairs={{0,4},{4,8},{8,12},{1,5},{5,9},{9,13},{2,6},{6,10},{10,14},{3,7},{... | collective-permute-start | bytes 12296 | tf_op jit(solution)/shard_map/ppermute | solution.py:19
  96.1 1.3 collective-permute-start.5
  97.4 3.0 %collective-permute-done.5 = bf16[1,16,128]{2,1,0:T(8,128)(2,1)S(1)} collective-permute-done((bf16[1,16,128]{2,1,0:T(8,128)(2,1)S(1)}, bf16[1,16,128]{2,1,0:T(8,128)(2,1)S(1)}, u32[]{:S(2)}, u32[]{:S(2)}) %collective-permute-start.5) | collective-permute-done | bytes 4128 | tf_op jit(solution)/shard_map/ppermute | solution.py:20
  100.4 3.4 %collective-permute-start.6 = (bf16[18,1,128]{2,1,0:T(2,128)(2,1)S(1)}, bf16[18,1,128]{2,1,0:T(2,128)(2,1)S(1)}, u32[]{:S(2)}, u32[]{:S(2)}) collective-permute-start(bf16[18,1,128]{2,1,0:T(2,128)(2,1)S(1)} %get-tuple-element.179), channel_id=1, source_target_pairs={{0,1},{1,2},{2,3},{4,5},{5,6},{6,7},{8,9},{9,10},{10,11},{12,13},{... | collective-permute-start | bytes 13832 | tf_op jit(solution)/shard_map/ppermute | solution.py:19
  103.8 1.9 %collective-permute-start.7 = (bf16[18,1,128]{2,1,0:T(2,128)(2,1)S(1)}, bf16[18,1,128]{2,1,0:T(2,128)(2,1)S(1)}, u32[]{:S(2)}, u32[]{:S(2)}) collective-permute-start(bf16[18,1,128]{2,1,0:T(2,128)(2,1)S(1)} %get-tuple-element.180), channel_id=1, source_target_pairs={{1,0},{2,1},{3,2},{5,4},{6,5},{7,6},{9,8},{10,9},{11,10},{13,12},{... | collective-permute-start | bytes 13832 | tf_op jit(solution)/shard_map/ppermute | solution.py:20
  106.0 2.9 %collective-permute-done.7 = bf16[18,1,128]{2,1,0:T(2,128)(2,1)S(1)} collective-permute-done((bf16[18,1,128]{2,1,0:T(2,128)(2,1)S(1)}, bf16[18,1,128]{2,1,0:T(2,128)(2,1)S(1)}, u32[]{:S(2)}, u32[]{:S(2)}) %collective-permute-start.7) | collective-permute-done | bytes 4640 | tf_op jit(solution)/shard_map/ppermute | solution.py:20
  110.2 2.1 %collective-permute-start.8 = (bf16[1,16,128]{2,1,0:T(8,128)(2,1)S(1)}, bf16[1,16,128]{2,1,0:T(8,128)(2,1)S(1)}, u32[]{:S(2)}, u32[]{:S(2)}) collective-permute-start(bf16[1,16,128]{2,1,0:T(8,128)(2,1)S(1)} %get-tuple-element.187), channel_id=1, source_target_pairs={{0,4},{4,8},{8,12},{1,5},{5,9},{9,13},{2,6},{6,10},{10,14},{3,7},{... | collective-permute-start | bytes 12296 | tf_op jit(solution)/shard_map/ppermute | solution.py:19
  112.3 1.3 collective-permute-start.9
  113.6 3.0 %collective-permute-done.9 = bf16[1,16,128]{2,1,0:T(8,128)(2,1)S(1)} collective-permute-done((bf16[1,16,128]{2,1,0:T(8,128)(2,1)S(1)}, bf16[1,16,128]{2,1,0:T(8,128)(2,1)S(1)}, u32[]{:S(2)}, u32[]{:S(2)}) %collective-permute-start.9) | collective-permute-done | bytes 4128 | tf_op jit(solution)/shard_map/ppermute | solution.py:20
  116.7 3.4 %collective-permute-start.10 = (bf16[18,1,128]{2,1,0:T(2,128)(2,1)S(1)}, bf16[18,1,128]{2,1,0:T(2,128)(2,1)S(1)}, u32[]{:S(2)}, u32[]{:S(2)}) collective-permute-start(bf16[18,1,128]{2,1,0:T(2,128)(2,1)S(1)} %get-tuple-element.175), channel_id=1, source_target_pairs={{0,1},{1,2},{2,3},{4,5},{5,6},{6,7},{8,9},{9,10},{10,11},{12,13},{... | collective-permute-start | bytes 13832 | tf_op jit(solution)/shard_map/ppermute | solution.py:19
  120.1 1.9 %collective-permute-start.11 = (bf16[18,1,128]{2,1,0:T(2,128)(2,1)S(1)}, bf16[18,1,128]{2,1,0:T(2,128)(2,1)S(1)}, u32[]{:S(2)}, u32[]{:S(2)}) collective-permute-start(bf16[18,1,128]{2,1,0:T(2,128)(2,1)S(1)} %get-tuple-element.176), channel_id=1, source_target_pairs={{1,0},{2,1},{3,2},{5,4},{6,5},{7,6},{9,8},{10,9},{11,10},{13,12},{... | collective-permute-start | bytes 13832 | tf_op jit(solution)/shard_map/ppermute | solution.py:20
  122.2 2.9 %collective-permute-done.11 = bf16[18,1,128]{2,1,0:T(2,128)(2,1)S(1)} collective-permute-done((bf16[18,1,128]{2,1,0:T(2,128)(2,1)S(1)}, bf16[18,1,128]{2,1,0:T(2,128)(2,1)S(1)}, u32[]{:S(2)}, u32[]{:S(2)}) %collective-permute-start.11) | collective-permute-done | bytes 4640 | tf_op jit(solution)/shard_map/ppermute | solution.py:20
  (132 shorter events, 16.5 us)
Async XLA Ops:
  6.5 66.3 %reduce-scatter.2.cloned.1.call-start = ((), (), s32[]{:S(2)}) async-start(), calls=%async_computation.1 | async-start | bytes 81920 | tf_op jit(solution)/shard_map/reduce_scatter | solution.py:116
  15.1 3.9 %copy-start.2 = (bf16[128,33]{0,1:T(8,128)(2,1)S(1)}, bf16[128,33]{0,1:T(8,128)(2,1)}, u32[]{:S(2)}) copy-start(bf16[128,33]{0,1:T(8,128)(2,1)} %param.18) | copy-start | bytes 25348
  15.1 3.9 %copy-start.3 = (bf16[16,128]{1,0:T(8,128)(2,1)S(1)}, bf16[16,128]{1,0:T(8,128)(2,1)}, u32[]{:S(2)}) copy-start(bf16[16,128]{1,0:T(8,128)(2,1)} %param.17) | copy-start | bytes 12292
  19.0 30.9 %copy-start.5 = (s32[1,4]{1,0:T(1,128)S(1)}, s32[1,4]{1,0:T(1,128)}, u32[]{:S(2)}) copy-start(s32[1,4]{1,0:T(1,128)} %param.16) | copy-start | bytes 52
  19.0 69.4 %copy-start.4 = (bf16[9,32,128]{2,1,0:T(8,128)(2,1)S(1)}, bf16[9,32,128]{2,1,0:T(8,128)(2,1)}, u32[]{:S(2)}) copy-start(bf16[9,32,128]{2,1,0:T(8,128)(2,1)} %param.19) | copy-start | bytes 221188
  73.6 2.6 %collective-permute-start = (bf16[1,16,32]{2,1,0:T(8,128)(2,1)S(1)}, bf16[1,16,32]{2,1,0:T(8,128)(2,1)S(1)}, u32[]{:S(2)}, u32[]{:S(2)}) collective-permute-start(bf16[1,16,32]{2,1,0:T(8,128)(2,1)S(1)} %get-tuple-element.195), channel_id=1, source_target_pairs={{0,4},{4,8},{8,12},{1,5},{5,9},{9,13},{2,6},{6,10},{10,14},{3,7},{... | collective-permute-start | bytes 3080 | tf_op jit(solution)/shard_map/ppermute | solution.py:19
  74.9 4.4 %collective-permute-start.1 = (bf16[1,16,32]{2,1,0:T(8,128)(2,1)S(1)}, bf16[1,16,32]{2,1,0:T(8,128)(2,1)S(1)}, u32[]{:S(2)}, u32[]{:S(2)}) collective-permute-start(bf16[1,16,32]{2,1,0:T(8,128)(2,1)S(1)} %get-tuple-element.196), channel_id=1, source_target_pairs={{4,0},{8,4},{12,8},{5,1},{9,5},{13,9},{6,2},{10,6},{14,10},{7,3},{... | collective-permute-start | bytes 3080 | tf_op jit(solution)/shard_map/ppermute | solution.py:20
  79.3 9.2 %collective-permute-start.2 = (bf16[18,1,32]{2,1,0:T(2,128)(2,1)S(1)}, bf16[18,1,32]{2,1,0:T(2,128)(2,1)S(1)}, u32[]{:S(2)}, u32[]{:S(2)}) collective-permute-start(bf16[18,1,32]{2,1,0:T(2,128)(2,1)S(1)} %get-tuple-element.183), channel_id=1, source_target_pairs={{0,1},{1,2},{2,3},{4,5},{5,6},{6,7},{8,9},{9,10},{10,11},{12,13},{... | collective-permute-start | bytes 3464 | tf_op jit(solution)/shard_map/ppermute | solution.py:19
  86.4 5.0 %collective-permute-start.3 = (bf16[18,1,32]{2,1,0:T(2,128)(2,1)S(1)}, bf16[18,1,32]{2,1,0:T(2,128)(2,1)S(1)}, u32[]{:S(2)}, u32[]{:S(2)}) collective-permute-start(bf16[18,1,32]{2,1,0:T(2,128)(2,1)S(1)} %get-tuple-element.184), channel_id=1, source_target_pairs={{1,0},{2,1},{3,2},{5,4},{6,5},{7,6},{9,8},{10,9},{11,10},{13,12},{... | collective-permute-start | bytes 3464 | tf_op jit(solution)/shard_map/ppermute | solution.py:20
  88.4 17.4 %copy-start = (bf16[9,128,128]{2,1,0:T(8,128)(2,1)S(1)}, bf16[9,128,128]{2,1,0:T(8,128)(2,1)}, u32[]{:S(2)}) copy-start(bf16[9,128,128]{2,1,0:T(8,128)(2,1)} %param.20) | copy-start | bytes 884740
  92.7 4.7 %collective-permute-start.4 = (bf16[1,16,128]{2,1,0:T(8,128)(2,1)S(1)}, bf16[1,16,128]{2,1,0:T(8,128)(2,1)S(1)}, u32[]{:S(2)}, u32[]{:S(2)}) collective-permute-start(bf16[1,16,128]{2,1,0:T(8,128)(2,1)S(1)} %get-tuple-element.191), channel_id=1, source_target_pairs={{0,4},{4,8},{8,12},{1,5},{5,9},{9,13},{2,6},{6,10},{10,14},{3,7},{... | collective-permute-start | bytes 12296 | tf_op jit(solution)/shard_map/ppermute | solution.py:19
  96.1 4.4 %collective-permute-start.5 = (bf16[1,16,128]{2,1,0:T(8,128)(2,1)S(1)}, bf16[1,16,128]{2,1,0:T(8,128)(2,1)S(1)}, u32[]{:S(2)}, u32[]{:S(2)}) collective-permute-start(bf16[1,16,128]{2,1,0:T(8,128)(2,1)S(1)} %get-tuple-element.192), channel_id=1, source_target_pairs={{4,0},{8,4},{12,8},{5,1},{9,5},{13,9},{6,2},{10,6},{14,10},{7,3},{... | collective-permute-start | bytes 12296 | tf_op jit(solution)/shard_map/ppermute | solution.py:20
  100.4 5.5 %collective-permute-start.6 = (bf16[18,1,128]{2,1,0:T(2,128)(2,1)S(1)}, bf16[18,1,128]{2,1,0:T(2,128)(2,1)S(1)}, u32[]{:S(2)}, u32[]{:S(2)}) collective-permute-start(bf16[18,1,128]{2,1,0:T(2,128)(2,1)S(1)} %get-tuple-element.179), channel_id=1, source_target_pairs={{0,1},{1,2},{2,3},{4,5},{5,6},{6,7},{8,9},{9,10},{10,11},{12,13},{... | collective-permute-start | bytes 13832 | tf_op jit(solution)/shard_map/ppermute | solution.py:19
  103.8 5.0 %collective-permute-start.7 = (bf16[18,1,128]{2,1,0:T(2,128)(2,1)S(1)}, bf16[18,1,128]{2,1,0:T(2,128)(2,1)S(1)}, u32[]{:S(2)}, u32[]{:S(2)}) collective-permute-start(bf16[18,1,128]{2,1,0:T(2,128)(2,1)S(1)} %get-tuple-element.180), channel_id=1, source_target_pairs={{1,0},{2,1},{3,2},{5,4},{6,5},{7,6},{9,8},{10,9},{11,10},{13,12},{... | collective-permute-start | bytes 13832 | tf_op jit(solution)/shard_map/ppermute | solution.py:20
  105.9 16.1 %copy-start.1 = (bf16[9,128,128]{2,1,0:T(8,128)(2,1)S(1)}, bf16[9,128,128]{2,1,0:T(8,128)(2,1)}, u32[]{:S(2)}) copy-start(bf16[9,128,128]{2,1,0:T(8,128)(2,1)} %param.21) | copy-start | bytes 884740
  110.2 3.5 %collective-permute-start.8 = (bf16[1,16,128]{2,1,0:T(8,128)(2,1)S(1)}, bf16[1,16,128]{2,1,0:T(8,128)(2,1)S(1)}, u32[]{:S(2)}, u32[]{:S(2)}) collective-permute-start(bf16[1,16,128]{2,1,0:T(8,128)(2,1)S(1)} %get-tuple-element.187), channel_id=1, source_target_pairs={{0,4},{4,8},{8,12},{1,5},{5,9},{9,13},{2,6},{6,10},{10,14},{3,7},{... | collective-permute-start | bytes 12296 | tf_op jit(solution)/shard_map/ppermute | solution.py:19
  112.3 4.4 %collective-permute-start.9 = (bf16[1,16,128]{2,1,0:T(8,128)(2,1)S(1)}, bf16[1,16,128]{2,1,0:T(8,128)(2,1)S(1)}, u32[]{:S(2)}, u32[]{:S(2)}) collective-permute-start(bf16[1,16,128]{2,1,0:T(8,128)(2,1)S(1)} %get-tuple-element.188), channel_id=1, source_target_pairs={{4,0},{8,4},{12,8},{5,1},{9,5},{13,9},{6,2},{10,6},{14,10},{7,3},{... | collective-permute-start | bytes 12296 | tf_op jit(solution)/shard_map/ppermute | solution.py:20
  116.7 5.5 %collective-permute-start.10 = (bf16[18,1,128]{2,1,0:T(2,128)(2,1)S(1)}, bf16[18,1,128]{2,1,0:T(2,128)(2,1)S(1)}, u32[]{:S(2)}, u32[]{:S(2)}) collective-permute-start(bf16[18,1,128]{2,1,0:T(2,128)(2,1)S(1)} %get-tuple-element.175), channel_id=1, source_target_pairs={{0,1},{1,2},{2,3},{4,5},{5,6},{6,7},{8,9},{9,10},{10,11},{12,13},{... | collective-permute-start | bytes 13832 | tf_op jit(solution)/shard_map/ppermute | solution.py:19
  120.1 5.0 %collective-permute-start.11 = (bf16[18,1,128]{2,1,0:T(2,128)(2,1)S(1)}, bf16[18,1,128]{2,1,0:T(2,128)(2,1)S(1)}, u32[]{:S(2)}, u32[]{:S(2)}) collective-permute-start(bf16[18,1,128]{2,1,0:T(2,128)(2,1)S(1)} %get-tuple-element.176), channel_id=1, source_target_pairs={{1,0},{2,1},{3,2},{5,4},{6,5},{7,6},{9,8},{10,9},{11,10},{13,12},{... | collective-permute-start | bytes 13832 | tf_op jit(solution)/shard_map/ppermute | solution.py:20
Sparse Core Ops, SparseCore 0:
  52.1 20.6 reduce-scatter.1
where the time goes:
time: 135 us; the launch traced here: 134 us
  waiting for transfers between devices  38.6 us (29%)
  starting transfers between devices  30.3 us (22%)
  local copies, waits for them, and re-layouts  22.4 us (17%)
  between operations  13.9 us (10%)
  blocking collectives  11.3 us (8%)
  matrix products  9.79 us (7%)
  other arithmetic  7.22 us (5%)
    reduce_scatter x1, waiting for transfers between devices, shards(): lax.psum_scatter((colour * jnp.exp(-front)).astype(jnp.bfloat16), 'depth'...  20.8 us
    ppermute x6, starting transfers between devices, padded_2(): before = lax.ppermute(last, axis, up)  20.7 us
    ppermute x6, waiting for transfers between devices, padded_2(): after = lax.ppermute(first, axis, down)  17.7 us
    all_gather x1, blocking collectives, shards(): all_depth = lax.all_gather(depth_sum, 'depth', axis=0, tiled=True)  11.3 us
    ppermute x6, starting transfers between devices, padded_2(): after = lax.ppermute(first, axis, down)  9.64 us
    reshape x1, local copies, waits for them, and re-layouts, shards(): brick_features.reshape(feat_count, windows, SAMPLES).transpose(1, 2, 0)  5.43 us
    dot_general x27, matrix products, convolve_valid(): jnp.dot(window, weights[tap], preferred_element_type=jnp.float32)  4.52 us
    gather x2, local copies, waits for them, and re-layouts, march_block(): jnp.take(table, following, axis=0)  3.91 us
  transfers between devices with their start and end apart: 13, of which 7 were waited for; matrix products, arithmetic and copies ran while one was open for 0% of the time, Pallas kernels for 0%

commit v1 on v0

--- a/solution.py
+++ b/solution.py
@@ -7,6 +7,20 @@
 SAMPLES = 16
 ROWS_OWN = 16
 COLS_DEV = 16
+
+
+def clear_target(incoming_x, comm_axis, pos_dim):
+    odd = lax.axis_size(comm_axis)
+    x_next = lax.axis_index(comm_axis)
+    n_now, main = (odd, x_next)
+    frame_out, kept_arr = (incoming_x, 1)
+    while kept_arr < n_now:
+        w1 = lax.ppermute(frame_out, comm_axis, tuple(((t, t ^ kept_arr) for t in range(n_now))))
+        local_now = jnp.concatenate([frame_out, w1], pos_dim)
+        latest = jnp.concatenate([w1, frame_out], pos_dim)
+        frame_out = jnp.where(main & kept_arr == 0, local_now, latest)
+        kept_arr = 2 * kept_arr
+    return frame_out
 
 
 def padded_2(x, sides, width):
@@ -109,7 +123,7 @@
     )
     colour = jnp.transpose(colour_blocks, (1, 0, 2)).reshape(colour_blocks.shape[1], total_rays)
     depth_sum = depth_blocks.reshape(1, total_rays)
-    all_depth = lax.all_gather(depth_sum, "depth", axis=0, tiled=True)
+    all_depth = clear_target(depth_sum, "depth", 0)
     my_rank = ranks[lax.axis_index("depth")]
     ahead = (ranks < my_rank).astype(jnp.float32)[None, :]
     front = jnp.dot(ahead, all_depth, precision=lax.Precision.HIGHEST)

time: 135 us -> 129 us (0.956)
  blocking collectives: 11.3 us -> 0 us
  starting transfers between devices: 30.3 us -> 35 us
    all_gather x1 -> x0, blocking collectives: 11.3 us -> none  [shards(): all_depth = lax.all_gather(depth_sum, 'depth', axis=0, tiled=True)]
    ppermute x0 -> x2, starting transfers between devices: none -> 4.73 us  [clear_target(): lax.ppermute(frame_out, comm_axis, tuple(((t, t ^ kept_arr) for t in rang...]
    ppermute x0 -> x2, waiting for transfers between devices: none -> 1.43 us  [clear_target(): lax.ppermute(frame_out, comm_axis, tuple(((t, t ^ kept_arr) for t in rang...]
  transfers between devices with their start and end apart: 13 -> 15, of which waited for: 7 -> 9; matrix products, arithmetic and copies ran while one was open for 0% -> 1% of each run, Pallas kernels for 0% -> 0%
where the time goes in v1:
time: 129 us
  waiting for transfers between devices  39.7 us (31%)
  starting transfers between devices  35 us (27%)
  local copies, waits for them, and re-layouts  22.5 us (17%)
  between operations  13.9 us (11%)
  matrix products  9.8 us (8%)
  other arithmetic  7.46 us (6%)
    ppermute x6, starting transfers between devices, padded_2(): before = lax.ppermute(last, axis, up)  20.6 us
    reduce_scatter x1, waiting for transfers between devices, shards(): lax.psum_scatter((colour * jnp.exp(-front)).astype(jnp.bfloat16), 'depth'...  20.5 us
    ppermute x6, waiting for transfers between devices, padded_2(): after = lax.ppermute(first, axis, down)  17.7 us
    ppermute x6, starting transfers between devices, padded_2(): after = lax.ppermute(first, axis, down)  9.64 us
    reshape x1, local copies, waits for them, and re-layouts, shards(): brick_features.reshape(feat_count, windows, SAMPLES).transpose(1, 2, 0)  5.44 us
    ppermute x2, starting transfers between devices, clear_target(): lax.ppermute(frame_out, comm_axis, tuple(((t, t ^ kept_arr) for t in rang...  4.73 us
    dot_general x27, matrix products, convolve_valid(): jnp.dot(window, weights[tap], preferred_element_type=jnp.float32)  4.52 us
    gather x2, local copies, waits for them, and re-layouts, march_block(): jnp.take(table, window_ids, axis=0)  3.91 us
  transfers between devices with their start and end apart: 15, of which 9 were waited for; matrix products, arithmetic and copies ran while one was open for 1% of the time, Pallas kernels for 0%

profile of v1, /device:TPU:1, one launch (start us, length us, event | category | flops | bytes accessed | tf_op | source)
XLA Modules:
  0.0 128.7 jit_solution(11361095207159921004)
XLA Ops:
  7.1 1.4 %reduce.10 = s32[1024]{0:T(1024)S(1)} reduce(s32[1,1,1024]{2,1,0:T(1,128)} %param.15, s32[]{:T(128)} %broadcast.430), dimensions={0,1}, to_apply=%param.15.reduce_sub_computation.3 | reduce | bytes 8196 | tf_op args[2]
  8.5 1.4 %reduce.11 = s32[1024]{0:T(1024)S(1)} reduce(s32[1,1,1024]{2,1,0:T(1,128)} %param.14, s32[]{:T(128)} %broadcast.430), dimensions={0,1}, to_apply=%param.14.reduce_sub_computation.3 | reduce | bytes 8196 | tf_op args[1]
  9.9 5.4 %reshape.274 = bf16[16,1024,16]{2,1,0:T(8,128)(2,1)} reshape(bf16[16,1,1,16384]{3,0,2,1:T(8,128)(2,1)} %param.13) | data formatting | bytes 1048576 | tf_op jit(solution)/shard_map/reshape | solution.py:85
  15.4 3.7 %copy.13 = bf16[1024,16,16]{0,2,1:T(8,128)(2,1)S(1)} copy(bf16[1024,16,16]{1,0,2:T(8,128)(2,1)} %bitcast.218) | data formatting | bytes 1048576 | tf_op jit(solution)/shard_map/transpose | solution.py:86
  19.3 19.6 %while.14 = (s32[]{:T(128)}, f32[2,32,512]{2,1,0:T(8,128)S(1)}, f32[2,512]{1,0:T(2,128)S(1)}, s32[2,512]{1,0:T(2,128)S(1)}, s32[2,512]{1,0:T(2,128)S(1)}, /*inde...) while((s32[]{:T(128)}, f32[2,32,512]{2,1,0:T(8,128)S(1)}, ...), condition=%wide.region_3.5_spmd, body=%wide.region_0.4_spmd.sunk | while | flops 110472448 | bytes 23171440 | solution.py:121
  19.4 2.0 %gather_fusion.1 = bf16[512,256]{1,0:T(8,128)(2,1)S(1)} fusion(bf16[1024,256]{1,0:T(8,128)(2,1)S(1)} %get-tuple-element.290, s32[1024]{0:T(1024)S(1)} %pad_clamp_fusion.5), kind=kCustom, calls=%fused_computation.clone.clone.1 | custom fusion | bytes 526336 | tf_op jit(solution)/shard_map/while/body/eval_jaxpr/jit(_take)/gather | solution.py:102
  21.5 2.0 %gather_fusion = bf16[512,256]{1,0:T(8,128)(2,1)S(1)} fusion(bf16[1024,256]{1,0:T(8,128)(2,1)S(1)} %get-tuple-element.290, s32[1024]{0:T(1024)S(1)} %pad_clamp_fusion.4), kind=kCustom, calls=%fused_computation.1.clone.clone.1 | custom fusion | bytes 526336 | tf_op jit(solution)/shard_map/while/body/eval_jaxpr/jit(_take)/gather | solution.py:102
  26.4 1.3 %convolution_bitcast_fusion.2 = f32[33,8192]{1,0:T(8,128)S(1)} fusion(bf16[128,8192]{0,1:T(8,128)(2,1)S(1)} %bitcast.215, bf16[128,33]{0,1:T(8,128)(2,1)S(1)} %get-tuple-element.292), kind=kOutput, calls=%fused_computation.2.clone.1 | convolution fusion | flops 69206016 | bytes 3186944 | tf_op jit(solution)/shard_map/while/body/eval_jaxpr/ho,hn->on/dot_general | solution.py:118
  29.2 2.0 %gather_fusion.1 = bf16[512,256]{1,0:T(8,128)(2,1)S(1)} fusion(bf16[1024,256]{1,0:T(8,128)(2,1)S(1)} %get-tuple-element.290, s32[1024]{0:T(1024)S(1)} %pad_clamp_fusion.5), kind=kCustom, calls=%fused_computation.clone.clone.1 | custom fusion | bytes 526336 | tf_op jit(solution)/shard_map/while/body/eval_jaxpr/jit(_take)/gather | solution.py:102
  31.3 2.0 %gather_fusion = bf16[512,256]{1,0:T(8,128)(2,1)S(1)} fusion(bf16[1024,256]{1,0:T(8,128)(2,1)S(1)} %get-tuple-element.290, s32[1024]{0:T(1024)S(1)} %pad_clamp_fusion.4), kind=kCustom, calls=%fused_computation.1.clone.clone.1 | custom fusion | bytes 526336 | tf_op jit(solution)/shard_map/while/body/eval_jaxpr/jit(_take)/gather | solution.py:102
  36.2 1.3 %convolution_bitcast_fusion.2 = f32[33,8192]{1,0:T(8,128)S(1)} fusion(bf16[128,8192]{0,1:T(8,128)(2,1)S(1)} %bitcast.215, bf16[128,33]{0,1:T(8,128)(2,1)S(1)} %get-tuple-element.292), kind=kOutput, calls=%fused_computation.2.clone.1 | convolution fusion | flops 69206016 | bytes 3186944 | tf_op jit(solution)/shard_map/while/body/eval_jaxpr/ho,hn->on/dot_general | solution.py:118
  38.9 2.2 %collective-permute-start = (f32[1,1024]{1,0:T(1,128)S(1)}, f32[1,1024]{1,0:T(1,128)S(1)}, u32[]{:S(2)}, u32[]{:S(2)}) collective-permute-start(f32[1,1024]{1,0:T(1,128)S(1)} %bitcast.260), channel_id=1, source_target_pairs={{0,4},{4,0},{8,12},{12,8},{1,5},{5,1},{9,13},{13,9},{2,6},{6,2},{1... | collective-permute-start | bytes 12296 | tf_op jit(solution)/shard_map/ppermute | solution.py:18
  42.1 2.5 %collective-permute-start.1 = (f32[2,1024]{1,0:T(2,128)S(1)}, f32[2,1024]{1,0:T(2,128)S(1)}, u32[]{:S(2)}, u32[]{:S(2)}) collective-permute-start(f32[2,1024]{1,0:T(2,128)S(1)} %maximum_select_fusion.2), channel_id=1, source_target_pairs={{0,8},{4,12},{8,0},{12,4},{1,9},{5,13},{9,1},{13,5},{2,10},{6,14},... | collective-permute-start | bytes 24584 | tf_op jit(solution)/shard_map/ppermute | solution.py:18
  47.2 20.5 %reduce-scatter.2.cloned.1.call-done = bf16[32,256]{1,0:T(8,128)(2,1)} async-done(((bf16[32,1024]{1,0:T(8,128)(2,1)}), bf16[32,256]{1,0:T(8,128)(2,1)}) %reduce-scatter.2.cloned.1.call-update) | async-done | bytes 16400 | tf_op jit(solution)/shard_map/reduce_scatter | solution.py:130
  68.5 1.3 %collective-permute-start.2 = (bf16[1,16,32]{2,1,0:T(8,128)(2,1)S(1)}, bf16[1,16,32]{2,1,0:T(8,128)(2,1)S(1)}, u32[]{:S(2)}, u32[]{:S(2)}) collective-permute-start(bf16[1,16,32]{2,1,0:T(8,128)(2,1)S(1)} %get-tuple-element.187), channel_id=1, source_target_pairs={{0,4},{4,8},{8,12},{1,5},{5,9},{9,13},{2,6},{6,10},{10,14},{3,7},{... | collective-permute-start | bytes 3080 | tf_op jit(solution)/shard_map/ppermute | solution.py:33
  69.8 1.3 %collective-permute-start.3 = (bf16[1,16,32]{2,1,0:T(8,128)(2,1)S(1)}, bf16[1,16,32]{2,1,0:T(8,128)(2,1)S(1)}, u32[]{:S(2)}, u32[]{:S(2)}) collective-permute-start(bf16[1,16,32]{2,1,0:T(8,128)(2,1)S(1)} %get-tuple-element.188), channel_id=1, source_target_pairs={{4,0},{8,4},{12,8},{5,1},{9,5},{13,9},{6,2},{10,6},{14,10},{7,3},{... | collective-permute-start | bytes 3080 | tf_op jit(solution)/shard_map/ppermute | solution.py:34
  71.1 3.0 %collective-permute-done.3 = bf16[1,16,32]{2,1,0:T(8,128)(2,1)S(1)} collective-permute-done((bf16[1,16,32]{2,1,0:T(8,128)(2,1)S(1)}, bf16[1,16,32]{2,1,0:T(8,128)(2,1)S(1)}, u32[]{:S(2)}, u32[]{:S(2)}) %collective-permute-start.3) | collective-permute-done | bytes 1056 | tf_op jit(solution)/shard_map/ppermute | solution.py:34
  74.2 7.1 %collective-permute-start.4 = (bf16[18,1,32]{2,1,0:T(2,128)(2,1)S(1)}, bf16[18,1,32]{2,1,0:T(2,128)(2,1)S(1)}, u32[]{:S(2)}, u32[]{:S(2)}) collective-permute-start(bf16[18,1,32]{2,1,0:T(2,128)(2,1)S(1)} %get-tuple-element.175), channel_id=1, source_target_pairs={{0,1},{1,2},{2,3},{4,5},{5,6},{6,7},{8,9},{9,10},{10,11},{12,13},{... | collective-permute-start | bytes 3464 | tf_op jit(solution)/shard_map/ppermute | solution.py:33
  81.3 1.9 %collective-permute-start.5 = (bf16[18,1,32]{2,1,0:T(2,128)(2,1)S(1)}, bf16[18,1,32]{2,1,0:T(2,128)(2,1)S(1)}, u32[]{:S(2)}, u32[]{:S(2)}) collective-permute-start(bf16[18,1,32]{2,1,0:T(2,128)(2,1)S(1)} %get-tuple-element.176), channel_id=1, source_target_pairs={{1,0},{2,1},{3,2},{5,4},{6,5},{7,6},{9,8},{10,9},{11,10},{13,12},{... | collective-permute-start | bytes 3464 | tf_op jit(solution)/shard_map/ppermute | solution.py:34
  83.4 2.9 %collective-permute-done.5 = bf16[18,1,32]{2,1,0:T(2,128)(2,1)S(1)} collective-permute-done((bf16[18,1,32]{2,1,0:T(2,128)(2,1)S(1)}, bf16[18,1,32]{2,1,0:T(2,128)(2,1)S(1)}, u32[]{:S(2)}, u32[]{:S(2)}) %collective-permute-start.5) | collective-permute-done | bytes 1184 | tf_op jit(solution)/shard_map/ppermute | solution.py:34
  87.5 3.4 %collective-permute-start.6 = (bf16[1,16,128]{2,1,0:T(8,128)(2,1)S(1)}, bf16[1,16,128]{2,1,0:T(8,128)(2,1)S(1)}, u32[]{:S(2)}, u32[]{:S(2)}) collective-permute-start(bf16[1,16,128]{2,1,0:T(8,128)(2,1)S(1)} %get-tuple-element.183), channel_id=1, source_target_pairs={{0,4},{4,8},{8,12},{1,5},{5,9},{9,13},{2,6},{6,10},{10,14},{3,7},{... | collective-permute-start | bytes 12296 | tf_op jit(solution)/shard_map/ppermute | solution.py:33
  91.0 1.3 %collective-permute-start.7 = (bf16[1,16,128]{2,1,0:T(8,128)(2,1)S(1)}, bf16[1,16,128]{2,1,0:T(8,128)(2,1)S(1)}, u32[]{:S(2)}, u32[]{:S(2)}) collective-permute-start(bf16[1,16,128]{2,1,0:T(8,128)(2,1)S(1)} %get-tuple-element.184), channel_id=1, source_target_pairs={{4,0},{8,4},{12,8},{5,1},{9,5},{13,9},{6,2},{10,6},{14,10},{7,3},{... | collective-permute-start | bytes 12296 | tf_op jit(solution)/shard_map/ppermute | solution.py:34
  92.3 3.0 %collective-permute-done.7 = bf16[1,16,128]{2,1,0:T(8,128)(2,1)S(1)} collective-permute-done((bf16[1,16,128]{2,1,0:T(8,128)(2,1)S(1)}, bf16[1,16,128]{2,1,0:T(8,128)(2,1)S(1)}, u32[]{:S(2)}, u32[]{:S(2)}) %collective-permute-start.7) | collective-permute-done | bytes 4128 | tf_op jit(solution)/shard_map/ppermute | solution.py:34
  95.3 3.4 %collective-permute-start.8 = (bf16[18,1,128]{2,1,0:T(2,128)(2,1)S(1)}, bf16[18,1,128]{2,1,0:T(2,128)(2,1)S(1)}, u32[]{:S(2)}, u32[]{:S(2)}) collective-permute-start(bf16[18,1,128]{2,1,0:T(2,128)(2,1)S(1)} %get-tuple-element.171), channel_id=1, source_target_pairs={{0,1},{1,2},{2,3},{4,5},{5,6},{6,7},{8,9},{9,10},{10,11},{12,13},{... | collective-permute-start | bytes 13832 | tf_op jit(solution)/shard_map/ppermute | solution.py:33
  98.7 1.9 %collective-permute-start.9 = (bf16[18,1,128]{2,1,0:T(2,128)(2,1)S(1)}, bf16[18,1,128]{2,1,0:T(2,128)(2,1)S(1)}, u32[]{:S(2)}, u32[]{:S(2)}) collective-permute-start(bf16[18,1,128]{2,1,0:T(2,128)(2,1)S(1)} %get-tuple-element.172), channel_id=1, source_target_pairs={{1,0},{2,1},{3,2},{5,4},{6,5},{7,6},{9,8},{10,9},{11,10},{13,12},{... | collective-permute-start | bytes 13832 | tf_op jit(solution)/shard_map/ppermute | solution.py:34
  100.8 2.9 %collective-permute-done.9 = bf16[18,1,128]{2,1,0:T(2,128)(2,1)S(1)} collective-permute-done((bf16[18,1,128]{2,1,0:T(2,128)(2,1)S(1)}, bf16[18,1,128]{2,1,0:T(2,128)(2,1)S(1)}, u32[]{:S(2)}, u32[]{:S(2)}) %collective-permute-start.9) | collective-permute-done | bytes 4640 | tf_op jit(solution)/shard_map/ppermute | solution.py:34
  105.1 2.1 %collective-permute-start.10 = (bf16[1,16,128]{2,1,0:T(8,128)(2,1)S(1)}, bf16[1,16,128]{2,1,0:T(8,128)(2,1)S(1)}, u32[]{:S(2)}, u32[]{:S(2)}) collective-permute-start(bf16[1,16,128]{2,1,0:T(8,128)(2,1)S(1)} %get-tuple-element.179), channel_id=1, source_target_pairs={{0,4},{4,8},{8,12},{1,5},{5,9},{9,13},{2,6},{6,10},{10,14},{3,7},{... | collective-permute-start | bytes 12296 | tf_op jit(solution)/shard_map/ppermute | solution.py:33
  107.2 1.3 %collective-permute-start.11 = (bf16[1,16,128]{2,1,0:T(8,128)(2,1)S(1)}, bf16[1,16,128]{2,1,0:T(8,128)(2,1)S(1)}, u32[]{:S(2)}, u32[]{:S(2)}) collective-permute-start(bf16[1,16,128]{2,1,0:T(8,128)(2,1)S(1)} %get-tuple-element.180), channel_id=1, source_target_pairs={{4,0},{8,4},{12,8},{5,1},{9,5},{13,9},{6,2},{10,6},{14,10},{7,3},{... | collective-permute-start | bytes 12296 | tf_op jit(solution)/shard_map/ppermute | solution.py:34
  108.5 3.0 %collective-permute-done.11 = bf16[1,16,128]{2,1,0:T(8,128)(2,1)S(1)} collective-permute-done((bf16[1,16,128]{2,1,0:T(8,128)(2,1)S(1)}, bf16[1,16,128]{2,1,0:T(8,128)(2,1)S(1)}, u32[]{:S(2)}, u32[]{:S(2)}) %collective-permute-start.11) | collective-permute-done | bytes 4128 | tf_op jit(solution)/shard_map/ppermute | solution.py:34
  111.5 3.4 %collective-permute-start.12 = (bf16[18,1,128]{2,1,0:T(2,128)(2,1)S(1)}, bf16[18,1,128]{2,1,0:T(2,128)(2,1)S(1)}, u32[]{:S(2)}, u32[]{:S(2)}) collective-permute-start(bf16[18,1,128]{2,1,0:T(2,128)(2,1)S(1)} %get-tuple-element.167), channel_id=1, source_target_pairs={{0,1},{1,2},{2,3},{4,5},{5,6},{6,7},{8,9},{9,10},{10,11},{12,13},{... | collective-permute-start | bytes 13832 | tf_op jit(solution)/shard_map/ppermute | solution.py:33
  114.9 1.9 %collective-permute-start.13 = (bf16[18,1,128]{2,1,0:T(2,128)(2,1)S(1)}, bf16[18,1,128]{2,1,0:T(2,128)(2,1)S(1)}, u32[]{:S(2)}, u32[]{:S(2)}) collective-permute-start(bf16[18,1,128]{2,1,0:T(2,128)(2,1)S(1)} %get-tuple-element.168), channel_id=1, source_target_pairs={{1,0},{2,1},{3,2},{5,4},{6,5},{7,6},{9,8},{10,9},{11,10},{13,12},{... | collective-permute-start | bytes 13832 | tf_op jit(solution)/shard_map/ppermute | solution.py:34
  117.0 2.9 %collective-permute-done.13 = bf16[18,1,128]{2,1,0:T(2,128)(2,1)S(1)} collective-permute-done((bf16[18,1,128]{2,1,0:T(2,128)(2,1)S(1)}, bf16[18,1,128]{2,1,0:T(2,128)(2,1)S(1)}, u32[]{:S(2)}, u32[]{:S(2)}) %collective-permute-start.13) | collective-permute-done | bytes 4640 | tf_op jit(solution)/shard_map/ppermute | solution.py:34
  (136 shorter events, 18.9 us)
Async XLA Ops:
  6.5 61.2 %reduce-scatter.2.cloned.1.call-start = ((), (), s32[]{:S(2)}) async-start(), calls=%async_computation.1 | async-start | bytes 81920 | tf_op jit(solution)/shard_map/reduce_scatter | solution.py:130
  15.4 3.9 %copy-start.2 = (bf16[128,33]{0,1:T(8,128)(2,1)S(1)}, bf16[128,33]{0,1:T(8,128)(2,1)}, u32[]{:S(2)}) copy-start(bf16[128,33]{0,1:T(8,128)(2,1)} %param.18) | copy-start | bytes 25348
  15.4 3.9 %copy-start.3 = (bf16[16,128]{1,0:T(8,128)(2,1)S(1)}, bf16[16,128]{1,0:T(8,128)(2,1)}, u32[]{:S(2)}) copy-start(bf16[16,128]{1,0:T(8,128)(2,1)} %param.17) | copy-start | bytes 12292
  19.3 25.4 %copy-start.5 = (s32[1,4]{1,0:T(1,128)S(1)}, s32[1,4]{1,0:T(1,128)}, u32[]{:S(2)}) copy-start(s32[1,4]{1,0:T(1,128)} %param.16) | copy-start | bytes 52
  19.3 63.9 %copy-start.4 = (bf16[9,32,128]{2,1,0:T(8,128)(2,1)S(1)}, bf16[9,32,128]{2,1,0:T(8,128)(2,1)}, u32[]{:S(2)}) copy-start(bf16[9,32,128]{2,1,0:T(8,128)(2,1)} %param.19) | copy-start | bytes 221188
  38.9 3.2 %collective-permute-start = (f32[1,1024]{1,0:T(1,128)S(1)}, f32[1,1024]{1,0:T(1,128)S(1)}, u32[]{:S(2)}, u32[]{:S(2)}) collective-permute-start(f32[1,1024]{1,0:T(1,128)S(1)} %bitcast.260), channel_id=1, source_target_pairs={{0,4},{4,0},{8,12},{12,8},{1,5},{5,1},{9,13},{13,9},{2,6},{6,2},{1... | collective-permute-start | bytes 12296 | tf_op jit(solution)/shard_map/ppermute | solution.py:18
  42.1 3.6 %collective-permute-start.1 = (f32[2,1024]{1,0:T(2,128)S(1)}, f32[2,1024]{1,0:T(2,128)S(1)}, u32[]{:S(2)}, u32[]{:S(2)}) collective-permute-start(f32[2,1024]{1,0:T(2,128)S(1)} %maximum_select_fusion.2), channel_id=1, source_target_pairs={{0,8},{4,12},{8,0},{12,4},{1,9},{5,13},{9,1},{13,5},{2,10},{6,14},... | collective-permute-start | bytes 24584 | tf_op jit(solution)/shard_map/ppermute | solution.py:18
  68.5 2.6 %collective-permute-start.2 = (bf16[1,16,32]{2,1,0:T(8,128)(2,1)S(1)}, bf16[1,16,32]{2,1,0:T(8,128)(2,1)S(1)}, u32[]{:S(2)}, u32[]{:S(2)}) collective-permute-start(bf16[1,16,32]{2,1,0:T(8,128)(2,1)S(1)} %get-tuple-element.187), channel_id=1, source_target_pairs={{0,4},{4,8},{8,12},{1,5},{5,9},{9,13},{2,6},{6,10},{10,14},{3,7},{... | collective-permute-start | bytes 3080 | tf_op jit(solution)/shard_map/ppermute | solution.py:33
  69.8 4.4 %collective-permute-start.3 = (bf16[1,16,32]{2,1,0:T(8,128)(2,1)S(1)}, bf16[1,16,32]{2,1,0:T(8,128)(2,1)S(1)}, u32[]{:S(2)}, u32[]{:S(2)}) collective-permute-start(bf16[1,16,32]{2,1,0:T(8,128)(2,1)S(1)} %get-tuple-element.188), channel_id=1, source_target_pairs={{4,0},{8,4},{12,8},{5,1},{9,5},{13,9},{6,2},{10,6},{14,10},{7,3},{... | collective-permute-start | bytes 3080 | tf_op jit(solution)/shard_map/ppermute | solution.py:34
  74.2 9.2 %collective-permute-start.4 = (bf16[18,1,32]{2,1,0:T(2,128)(2,1)S(1)}, bf16[18,1,32]{2,1,0:T(2,128)(2,1)S(1)}, u32[]{:S(2)}, u32[]{:S(2)}) collective-permute-start(bf16[18,1,32]{2,1,0:T(2,128)(2,1)S(1)} %get-tuple-element.175), channel_id=1, source_target_pairs={{0,1},{1,2},{2,3},{4,5},{5,6},{6,7},{8,9},{9,10},{10,11},{12,13},{... | collective-permute-start | bytes 3464 | tf_op jit(solution)/shard_map/ppermute | solution.py:33
  81.3 5.0 %collective-permute-start.5 = (bf16[18,1,32]{2,1,0:T(2,128)(2,1)S(1)}, bf16[18,1,32]{2,1,0:T(2,128)(2,1)S(1)}, u32[]{:S(2)}, u32[]{:S(2)}) collective-permute-start(bf16[18,1,32]{2,1,0:T(2,128)(2,1)S(1)} %get-tuple-element.176), channel_id=1, source_target_pairs={{1,0},{2,1},{3,2},{5,4},{6,5},{7,6},{9,8},{10,9},{11,10},{13,12},{... | collective-permute-start | bytes 3464 | tf_op jit(solution)/shard_map/ppermute | solution.py:34
  83.3 17.4 %copy-start = (bf16[9,128,128]{2,1,0:T(8,128)(2,1)S(1)}, bf16[9,128,128]{2,1,0:T(8,128)(2,1)}, u32[]{:S(2)}) copy-start(bf16[9,128,128]{2,1,0:T(8,128)(2,1)} %param.20) | copy-start | bytes 884740
  87.5 4.7 %collective-permute-start.6 = (bf16[1,16,128]{2,1,0:T(8,128)(2,1)S(1)}, bf16[1,16,128]{2,1,0:T(8,128)(2,1)S(1)}, u32[]{:S(2)}, u32[]{:S(2)}) collective-permute-start(bf16[1,16,128]{2,1,0:T(8,128)(2,1)S(1)} %get-tuple-element.183), channel_id=1, source_target_pairs={{0,4},{4,8},{8,12},{1,5},{5,9},{9,13},{2,6},{6,10},{10,14},{3,7},{... | collective-permute-start | bytes 12296 | tf_op jit(solution)/shard_map/ppermute | solution.py:33
  91.0 4.4 %collective-permute-start.7 = (bf16[1,16,128]{2,1,0:T(8,128)(2,1)S(1)}, bf16[1,16,128]{2,1,0:T(8,128)(2,1)S(1)}, u32[]{:S(2)}, u32[]{:S(2)}) collective-permute-start(bf16[1,16,128]{2,1,0:T(8,128)(2,1)S(1)} %get-tuple-element.184), channel_id=1, source_target_pairs={{4,0},{8,4},{12,8},{5,1},{9,5},{13,9},{6,2},{10,6},{14,10},{7,3},{... | collective-permute-start | bytes 12296 | tf_op jit(solution)/shard_map/ppermute | solution.py:34
  95.3 5.5 %collective-permute-start.8 = (bf16[18,1,128]{2,1,0:T(2,128)(2,1)S(1)}, bf16[18,1,128]{2,1,0:T(2,128)(2,1)S(1)}, u32[]{:S(2)}, u32[]{:S(2)}) collective-permute-start(bf16[18,1,128]{2,1,0:T(2,128)(2,1)S(1)} %get-tuple-element.171), channel_id=1, source_target_pairs={{0,1},{1,2},{2,3},{4,5},{5,6},{6,7},{8,9},{9,10},{10,11},{12,13},{... | collective-permute-start | bytes 13832 | tf_op jit(solution)/shard_map/ppermute | solution.py:33
  98.7 5.0 %collective-permute-start.9 = (bf16[18,1,128]{2,1,0:T(2,128)(2,1)S(1)}, bf16[18,1,128]{2,1,0:T(2,128)(2,1)S(1)}, u32[]{:S(2)}, u32[]{:S(2)}) collective-permute-start(bf16[18,1,128]{2,1,0:T(2,128)(2,1)S(1)} %get-tuple-element.172), channel_id=1, source_target_pairs={{1,0},{2,1},{3,2},{5,4},{6,5},{7,6},{9,8},{10,9},{11,10},{13,12},{... | collective-permute-start | bytes 13832 | tf_op jit(solution)/shard_map/ppermute | solution.py:34
  100.8 16.1 %copy-start.1 = (bf16[9,128,128]{2,1,0:T(8,128)(2,1)S(1)}, bf16[9,128,128]{2,1,0:T(8,128)(2,1)}, u32[]{:S(2)}) copy-start(bf16[9,128,128]{2,1,0:T(8,128)(2,1)} %param.21) | copy-start | bytes 884740
  105.1 3.4 %collective-permute-start.10 = (bf16[1,16,128]{2,1,0:T(8,128)(2,1)S(1)}, bf16[1,16,128]{2,1,0:T(8,128)(2,1)S(1)}, u32[]{:S(2)}, u32[]{:S(2)}) collective-permute-start(bf16[1,16,128]{2,1,0:T(8,128)(2,1)S(1)} %get-tuple-element.179), channel_id=1, source_target_pairs={{0,4},{4,8},{8,12},{1,5},{5,9},{9,13},{2,6},{6,10},{10,14},{3,7},{... | collective-permute-start | bytes 12296 | tf_op jit(solution)/shard_map/ppermute | solution.py:33
  107.2 4.4 %collective-permute-start.11 = (bf16[1,16,128]{2,1,0:T(8,128)(2,1)S(1)}, bf16[1,16,128]{2,1,0:T(8,128)(2,1)S(1)}, u32[]{:S(2)}, u32[]{:S(2)}) collective-permute-start(bf16[1,16,128]{2,1,0:T(8,128)(2,1)S(1)} %get-tuple-element.180), channel_id=1, source_target_pairs={{4,0},{8,4},{12,8},{5,1},{9,5},{13,9},{6,2},{10,6},{14,10},{7,3},{... | collective-permute-start | bytes 12296 | tf_op jit(solution)/shard_map/ppermute | solution.py:34
  111.5 5.5 %collective-permute-start.12 = (bf16[18,1,128]{2,1,0:T(2,128)(2,1)S(1)}, bf16[18,1,128]{2,1,0:T(2,128)(2,1)S(1)}, u32[]{:S(2)}, u32[]{:S(2)}) collective-permute-start(bf16[18,1,128]{2,1,0:T(2,128)(2,1)S(1)} %get-tuple-element.167), channel_id=1, source_target_pairs={{0,1},{1,2},{2,3},{4,5},{5,6},{6,7},{8,9},{9,10},{10,11},{12,13},{... | collective-permute-start | bytes 13832 | tf_op jit(solution)/shard_map/ppermute | solution.py:33
  114.9 5.0 %collective-permute-start.13 = (bf16[18,1,128]{2,1,0:T(2,128)(2,1)S(1)}, bf16[18,1,128]{2,1,0:T(2,128)(2,1)S(1)}, u32[]{:S(2)}, u32[]{:S(2)}) collective-permute-start(bf16[18,1,128]{2,1,0:T(2,128)(2,1)S(1)} %get-tuple-element.168), channel_id=1, source_target_pairs={{1,0},{2,1},{3,2},{5,4},{6,5},{7,6},{9,8},{10,9},{11,10},{13,12},{... | collective-permute-start | bytes 13832 | tf_op jit(solution)/shard_map/ppermute | solution.py:34
Sparse Core Ops, SparseCore 0:
  47.3 20.3 reduce-scatter.1
